TPU v7x, 32 devices: a whole 2x2x4 slice. The times are simulated.
32 devices in a mesh: tile: 8 (over y, x, core), corner: 4 (over z).
Axes of the slice: x: 2, y: 2, z: 4, core: 2. Of those that a mesh axis runs over, the one named last changes fastest.
Arguments:
- mask: float32 [1024, 384], P('tile'), may hold values from 0 to 1
- target: int32 [1024, 384], P('tile'), may hold values 0 or 1
- pixel_weight: float32 [1024, 384], P('tile'), may hold values from 0.49 to 108
- row_taps: float32 [4, 8, 2, 129], replicated, may hold values from -2 to 2
- col_taps: float32 [4, 8, 2, 129], replicated, may hold values from -2 to 2
- kernel_weights: float32 [4, 8], replicated, may hold values from 0.03 to 0.25
- corner_set: int32 [16], P('corner'), may hold values from 0 to 3
- dose: float32 [16], P('corner'), may hold values from 0.8 to 1.25
Outputs:
- soft_error: float32 [1024, 384], P('tile')
- new_mask: float32 [1024, 384], P(('tile', 'corner'))
Inputs may be any that keep to these rules, and one draw needn't show every extreme that they name: `corner_set`: each corner names one of 4 focus settings. target pixels are 0 or 1.
All inputs are finite; a program needn't handle non-finite values. No bound on the sum of `target` on one device may be relied on, other than what follows from the above.
Results may differ from a plain program's by a relative error of at most 0.0051.
Values may be sent and summed in bfloat16 or wider, within the bound.
A program may use at most 64 MiB of HBM per device.

v0:
```python
import jax
import jax.numpy as jnp
from jax import lax
from jax.sharding import PartitionSpec as P

block_cols = 128
lse_sharp = 6.0
print_steep = 3.0
print_level = 1.0
step_rate = 0.25
small_eps = 1e-06


def with_halo(value, sides, width):
    for axis, dim in sides:
        count, length = (lax.axis_size(axis), value.shape[dim])
        up = [(i, (i + 1) % count) for i in range(count - 1)]
        down = [(j, i) for i, j in up]
        last = lax.slice_in_dim(value, length - width, length, axis=dim)
        leading = lax.slice_in_dim(value, 0, width, axis=dim)
        before = lax.ppermute(last, axis, up)
        after = lax.ppermute(leading, axis, down)
        value = jnp.concatenate([before, value, after], axis=dim)
    return value


def passed_along(value, axis, steps):
    count = lax.axis_size(axis)
    leading, last = (max(0, -steps), min(count, count - steps))
    return lax.ppermute(value, axis, [(source, source + steps) for source in range(leading, last)])


def toeplitz(tap_values, row_count):
    leading = tap_values.shape[:-1]
    span_width = row_count + tap_values.shape[-1] - 1
    padded = jnp.concatenate(
        [tap_values, jnp.zeros(leading + (row_count,), tap_values.dtype)], axis=-1
    )
    repeated = jnp.tile(padded, (1,) * len(leading) + (row_count,))
    return repeated[..., : row_count * span_width].reshape(leading + (row_count, span_width))


def column_filter(masked, band_matrix):
    reach_cols = (band_matrix.shape[-1] - block_cols) // 2
    col_count = masked.shape[1]
    padded = jnp.pad(masked, ((0, 0), (reach_cols, reach_cols)))
    windows = jnp.stack(
        [
            padded[:, b * block_cols : b * block_cols + block_cols + 2 * reach_cols]
            for b in range(col_count // block_cols)
        ],
        axis=0,
    )
    product = jnp.einsum("bri,poi->prbo", windows, band_matrix, preferred_element_type=jnp.float32)
    return product.reshape(2, masked.shape[0], col_count)


def row_filter(band_matrix, cfield):
    product = jnp.einsum("aij,bjx->abix", band_matrix, cfield, preferred_element_type=jnp.float32)
    return (product[0, 0] - product[1, 1], product[0, 1] + product[1, 0])


def row_adjoint(band_matrix, cotangent):
    product = jnp.einsum(
        "aij,bix->abjx", band_matrix, cotangent, preferred_element_type=jnp.float32
    )
    return jnp.stack([product[0, 0] + product[1, 1], product[0, 1] - product[1, 0]])


def column_adjoint(back_field, band_matrix):
    reach_cols = (band_matrix.shape[-1] - block_cols) // 2
    line_count = back_field.shape[1]
    col_count = back_field.shape[2]
    blocks = back_field.reshape(2, line_count, col_count // block_cols, block_cols)
    pieces = jnp.einsum("prbo,poi->bri", blocks, band_matrix, preferred_element_type=jnp.float32)
    summed = jnp.zeros((line_count, col_count + 2 * reach_cols), jnp.float32)
    for b in range(col_count // block_cols):
        summed = summed.at[:, b * block_cols : b * block_cols + block_cols + 2 * reach_cols].add(
            pieces[b]
        )
    return summed[:, reach_cols : reach_cols + col_count]


def local(mask, target, pixel_weight, row_taps, col_taps, kernel_weights, corner_set, dose):
    row_count, col_count = mask.shape
    reach_rows = (row_taps.shape[-1] - 1) // 2
    set_count = row_taps.shape[0]
    masked = mask.astype(jnp.bfloat16)
    extended = with_halo(masked, (("tile", 0),), reach_rows)
    target_value = target.astype(jnp.float32)
    exp_total = jnp.zeros((row_count, col_count), jnp.float32)
    corner_states = []
    for c in range(corner_set.shape[0]):
        chosen = (jnp.arange(set_count, dtype=jnp.int32) == corner_set[c]).astype(jnp.float32)
        row_values = jnp.sum(chosen[:, None, None, None] * row_taps, axis=0)
        col_values = jnp.sum(chosen[:, None, None, None] * col_taps, axis=0)
        weights = jnp.sum(chosen[:, None] * kernel_weights, axis=0)
        row_bands = toeplitz(row_values.astype(jnp.bfloat16), row_count)
        col_bands = toeplitz(col_values.astype(jnp.bfloat16), block_cols)

        def forward(running, inputs):
            row_band, col_band, kernel_weight = inputs
            cfield = column_filter(extended, col_band).astype(jnp.bfloat16)
            field_real, field_imag = row_filter(row_band, cfield)
            running = running + kernel_weight * (field_real * field_real + field_imag * field_imag)
            return (running, jnp.stack([field_real, field_imag]).astype(jnp.bfloat16))

        summed, fields = lax.scan(
            forward, jnp.zeros((row_count, col_count), jnp.float32), (row_bands, col_bands, weights)
        )
        intensity = dose[c] * summed
        printed = jax.nn.sigmoid(print_steep * (intensity - print_level))
        differ = printed - target_value
        exp_error = jnp.exp(lse_sharp * (differ * differ))
        exp_total = exp_total + exp_error
        corner_states.append((row_bands, col_bands, weights, fields, printed, exp_error, dose[c]))
    denominator = lax.psum(exp_total.astype(jnp.bfloat16), "corner").astype(jnp.float32)
    soft_error = jnp.log(denominator) / lse_sharp
    grad_ext = jnp.zeros((row_count + 2 * reach_rows, col_count), jnp.float32)
    for corner_state in corner_states:
        row_bands, col_bands, weights, fields, printed, exp_error, corner_dose = corner_state
        slope = (
            pixel_weight
            * (exp_error / denominator)
            * (2.0 * (printed - target_value))
            * printed
            * (1.0 - printed)
            * print_steep
        )
        factor = 2.0 * corner_dose * slope

        def backward(running, inputs):
            row_band, col_band, kernel_weight, field_pair = inputs
            cotangent = (factor * kernel_weight * field_pair).astype(jnp.bfloat16)
            back_field = row_adjoint(row_band, cotangent).astype(jnp.bfloat16)
            return (running + column_adjoint(back_field, col_band), None)

        grad_ext, _ = lax.scan(backward, grad_ext, (row_bands, col_bands, weights, fields))
    upper_rim = grad_ext[:reach_rows]
    lower_rim = grad_ext[row_count + reach_rows :]
    middle = grad_ext[reach_rows : row_count + reach_rows]
    from_below = passed_along(upper_rim, "tile", -1)
    from_above = passed_along(lower_rim, "tile", 1)
    gradient = (
        middle
        + jnp.pad(from_above, ((0, row_count - reach_rows), (0, 0)))
        + jnp.pad(from_below, ((row_count - reach_rows, 0), (0, 0)))
    )
    share_rows = row_count // lax.axis_size("corner")
    first_row = lax.axis_index("corner") * share_rows
    own_mask = lax.dynamic_slice_in_dim(mask, first_row, share_rows, 0)
    pixel_count = row_count * lax.axis_size("tile") * col_count
    summed_grad = lax.psum(gradient, "corner")
    square = lax.psum(jnp.sum(summed_grad * summed_grad), "tile")
    own_rows = lax.dynamic_slice_in_dim(summed_grad, first_row, share_rows, 0)
    root_mean = jnp.sqrt(square / pixel_count + small_eps)
    new_mask = jnp.clip(own_mask - step_rate / root_mean * own_rows, 0.0, 1.0)
    return (soft_error, new_mask)


def solution(mesh):
    placed = (
        P("tile", None),
        P("tile", None),
        P("tile", None),
        P(),
        P(),
        P(),
        P("corner"),
        P("corner"),
    )
    return jax.shard_map(
        local,
        mesh=mesh,
        in_specs=placed,
        out_specs=(P("tile", None), P(("tile", "corner"), None)),
        check_vma=False,
    )
```

profile of v0, /device:TPU:0, one launch (start us, length us, event | category | flops | bytes accessed | tf_op | source)
XLA Modules:
  0.0 593.3 jit_solution(7374306210661256130)
XLA Ops:
  9.4 3.0 collective-permute-start
  27.0 3.1 tile.87
  32.7 3.1 tile.37
  38.4 3.1 tile.39
  44.2 3.1 tile.81
  50.8 3.1 tile.83
  56.5 3.1 tile.33
  62.1 3.1 tile.35
  68.8 49.2 %while.135 = (s32[]{:T(128)}, f32[128,384]{0,1:T(8,128)}, bf16[8,2,128,384]{2,3,0,1:T(8,128)(2,1)}, f32[8]{0:T(128)S(1)}, bf16[8,2,128,256]{3,2,1,0:T(8,128)(2,1...) while((s32[]{:T(128)}, f32[128,384]{0,1:T(8,128)}, ...), condition=%wide.region_19.20_spmd.clone, body=%wide.region_18.19_spmd.clone.sunk | while | flops 203685888 | bytes 5506679 | solution.py:108
  78.1 2.3 bitcast_add_fusion.11
  115.6 2.3 bitcast_add_fusion.11
  121.2 49.1 %while.133 = (s32[]{:T(128)}, f32[128,384]{0,1:T(8,128)}, bf16[8,2,128,384]{2,3,0,1:T(8,128)(2,1)}, f32[8]{0:T(128)S(1)}, bf16[8,2,128,256]{3,2,1,0:T(8,128)(2,1...) while((s32[]{:T(128)}, f32[128,384]{0,1:T(8,128)}, ...), condition=%wide.region_9.10_spmd.clone, body=%wide.region_8.9_spmd.clone.sunk | while | flops 203685888 | bytes 5506679 | solution.py:108
  173.5 38.1 %while.134 = (s32[]{:T(128)}, f32[128,384]{0,1:T(8,128)S(1)}, bf16[8,2,128,384]{2,3,0,1:T(8,128)(2,1)}, f32[8]{0:T(128)S(1)}, bf16[8,2,128,256]{3,2,1,0:T(8,128)...) while((s32[]{:T(128)}, f32[128,384]{0,1:T(8,128)S(1)}, ...), condition=%wide.region_14.15_spmd.clone, body=%wide.region_13.14_spmd.clone.sunk | while | flops 203685888 | bytes 5506679 | solution.py:108
  213.8 38.2 %while.132 = (s32[]{:T(128)}, f32[128,384]{0,1:T(8,128)S(1)}, bf16[8,2,128,384]{2,3,0,1:T(8,128)(2,1)}, f32[8]{0:T(128)S(1)}, bf16[8,2,128,256]{3,2,0,1:T(8,128)...) while((s32[]{:T(128)}, f32[128,384]{0,1:T(8,128)S(1)}, ...), condition=%wide.region_4.5_spmd.clone, body=%wide.region_3.4_spmd.clone.sunk | while | flops 203685888 | bytes 5506679 | solution.py:108
  252.1 4.9 add_convert_fusion
  265.0 30.6 %all-reduce.21.cloned.1.call-done = bf16[128,384]{1,0:T(8,128)(2,1)} async-done(((bf16[128,384]{1,0:T(8,128)(2,1)}), bf16[128,384]{1,0:T(8,128)(2,1)}) %all-reduce.21.cloned.1.call-update) | async-done | bytes 98320 | tf_op jit(solution)/shard_map/psum | solution.py:117
  295.5 5.0 fusion.160
  300.6 58.7 %while.136 = (s32[]{:T(128)}, f32[256,384]{0,1:T(8,128)S(1)}, bf16[8,2,128,256]{3,2,0,1:T(8,128)(2,1)}, f32[8]{0:T(128)S(1)}, f32[128,384]{0,1:T(8,128)S(1)}, /*...) while((s32[]{:T(128)}, f32[256,384]{0,1:T(8,128)S(1)}, ...), condition=%wide.region_25.26_spmd.clone, body=%wide.region_23.25_spmd.clone.sunk | while | flops 203374592 | bytes 10618519 | solution.py:138
  360.4 56.3 %while.129 = (s32[]{:T(128)}, f32[256,384]{0,1:T(8,128)S(1)}, bf16[8,2,128,256]{2,3,1,0:T(8,128)(2,1)}, f32[8]{0:T(128)S(1)}, f32[128,384]{0,1:T(8,128)S(1)}, /*...) while((s32[]{:T(128)}, f32[256,384]{0,1:T(8,128)S(1)}, ...), condition=%wide.region_28.29_spmd, body=%wide.region_26.28_spmd.sunk | while | flops 203276288 | bytes 10618501 | solution.py:138
  417.8 57.5 %while.130 = (s32[]{:T(128)}, f32[256,384]{0,1:T(8,128)S(1)}, bf16[8,2,128,256]{2,3,1,0:T(8,128)(2,1)}, f32[8]{0:T(128)S(1)}, f32[128,384]{0,1:T(8,128)S(1)}, /*...) while((s32[]{:T(128)}, f32[256,384]{0,1:T(8,128)S(1)}, ...), condition=%wide.region_31.32_spmd, body=%wide.region_29.31_spmd.sunk | while | flops 203276288 | bytes 10618501 | solution.py:138
  475.4 50.3 %while.131 = (s32[]{:T(128)}, f32[256,384]{0,1:T(8,128)S(1)}, bf16[8,2,128,256]{2,3,1,0:T(8,128)(2,1)S(1)}, f32[8]{0:T(128)S(1)}, f32[128,384]{0,1:T(8,128)S(1)}...) while((s32[]{:T(128)}, f32[256,384]{0,1:T(8,128)S(1)}, ...), condition=%wide.region_34.35_spmd, body=%wide.region_32.34_spmd.sunk | while | flops 203276288 | bytes 10617993 | solution.py:138
  528.5 3.5 collective-permute-done.3
  532.7 37.5 %all-reduce.23.cloned.1.call-done = f32[128,384]{1,0:T(8,128)} async-done(((f32[128,384]{1,0:T(8,128)}), f32[128,384]{1,0:T(8,128)}) %all-reduce.23.cloned.1.call-update) | async-done | bytes 196624 | tf_op jit(solution)/shard_map/psum | solution.py:153
  571.8 12.4 %psum.23 = f32[]{:T(128)} all-reduce(f32[]{:T(128)} %multiply_reduce_fusion), channel_id=1, replica_groups=mesh['tile'=8,'corner'=4] {'tile'}, use_global_device_ids=true, to_apply=%region_37.38 | all-reduce | flops 1 | bytes 8 | tf_op jit(solution)/shard_map/psum | solution.py:154
  (758 shorter events, 448.9 us)
Async XLA Ops:
  7.2 288.4 %all-reduce.21.cloned.1.call-start = ((), (), s32[]{:S(2)}) async-start(), calls=%async_computation | async-start | bytes 196608 | tf_op jit(solution)/shard_map/psum | solution.py:117
  8.2 0.6 copy-start.7
  9.4 57.1 %collective-permute-start = (bf16[64,384]{1,0:T(8,128)(2,1)}, bf16[64,384]{1,0:T(8,128)(2,1)}, u32[]{:S(2)}, u32[]{:S(2)}) collective-permute-start(bf16[64,384]{1,0:T(8,128)(2,1)} %get-tuple-element.1630), channel_id=1, source_target_pairs={{0,4},{4,8},{8,12},{12,16},{16,20},{20,24},{24,28},{1,5},{5,9},{9,... | collective-permute-start | bytes 147464 | tf_op jit(solution)/shard_map/ppermute | solution.py:21
  12.4 54.1 %collective-permute-start.1 = (bf16[64,384]{1,0:T(8,128)(2,1)}, bf16[64,384]{1,0:T(8,128)(2,1)}, u32[]{:S(2)}, u32[]{:S(2)}) collective-permute-start(bf16[64,384]{1,0:T(8,128)(2,1)} %get-tuple-element.1631), channel_id=1, source_target_pairs={{4,0},{8,4},{12,8},{16,12},{20,16},{24,20},{28,24},{5,1},{9,5},{13... | collective-permute-start | bytes 147464 | tf_op jit(solution)/shard_map/ppermute | solution.py:22
  30.1 1.2 copy-start.13
  35.9 1.2 copy-start.12
  41.5 1.3 copy-start.11
  47.3 1.0 copy-start
  48.3 1.2 copy-start.10
  53.9 1.2 copy-start.9
  65.3 1.2 copy-start.8
  118.0 3.2 copy-start.15
  170.3 3.2 copy-start.14
  211.5 2.3 copy-start.16
  252.1 7.0 %copy-start.5 = (f32[128,384]{1,0:T(8,128)}, f32[128,384]{1,0:T(8,128)S(1)}, u32[]{:S(2)}) copy-start(f32[128,384]{1,0:T(8,128)S(1)} %copy.88) | copy-start | bytes 589828
  252.1 9.4 %copy-start.1 = (bf16[8,2,32768]{2,0,1:T(8,128)(2,1)S(1)}, bf16[8,2,32768]{2,0,1:T(8,128)(2,1)}, u32[]{:S(2)}) copy-start(bf16[8,2,32768]{2,0,1:T(8,128)(2,1)} %copy-done) | copy-start | bytes 3145732
  257.1 313.2 %all-reduce.23.cloned.1.call-start = ((), (), s32[]{:S(2)}) async-start(), calls=%async_computation.1 | async-start | bytes 393216 | tf_op jit(solution)/shard_map/psum | solution.py:153
  263.2 32.3 %copy-start.2 = (f32[128,384]{1,0:T(8,128)S(1)}, f32[128,384]{1,0:T(8,128)}, u32[]{:S(2)}) copy-start(f32[128,384]{1,0:T(8,128)} %copy.103) | copy-start | bytes 589828
  263.2 32.3 %copy-start.3 = (f32[128,384]{1,0:T(8,128)S(1)}, f32[128,384]{1,0:T(8,128)}, u32[]{:S(2)}) copy-start(f32[128,384]{1,0:T(8,128)} %copy.93) | copy-start | bytes 589828
  263.2 32.3 %copy-start.4 = (f32[128,384]{1,0:T(8,128)S(1)}, f32[128,384]{1,0:T(8,128)}, u32[]{:S(2)}) copy-start(f32[128,384]{1,0:T(8,128)} %copy.98) | copy-start | bytes 589828
  263.2 32.3 %copy-start.6 = (f32[128,384]{1,0:T(8,128)S(1)}, f32[128,384]{1,0:T(8,128)}, u32[]{:S(2)}) copy-start(f32[128,384]{1,0:T(8,128)} %copy-done.5) | copy-start | bytes 589828
  525.9 2.6 collective-permute-start.2
  527.2 4.8 collective-permute-start.3
Sparse Core Ops, SparseCore 0:
  257.2 38.2 all-reduce.20
  532.9 37.3 all-reduce.22
where the time goes:
time: 598 us; the launch traced here: 593 us
  other arithmetic  208 us (35%)
  matrix products  152 us (25%)
  local copies, waits for them, and re-layouts  121 us (20%)
  waiting for transfers between devices  71.6 us (12%)
  between operations  17.8 us (3%)
  blocking collectives  12.4 us (2%)
  starting transfers between devices  6.91 us (1%)
    add x32, other arithmetic, forward(): running + kernel_weight * (field_real * field_real + field_imag * field_i...  48.1 us
    scatter-add x64, other arithmetic, column_adjoint(): summed.at[:, b * block_cols:b * block_cols + block_cols + 2 * reach_cols]  47.9 us
    another operation x129, other arithmetic  45.9 us
    dot_general x32, matrix products, row_adjoint(): jnp.einsum('aij,bix->abjx', band_matrix, cotangent, preferred_element_typ...  43.4 us
    dot_general x32, matrix products, column_filter(): jnp.einsum('bri,poi->prbo', windows, band_matrix, preferred_element_type=...  38.8 us
    dot_general x32, matrix products, row_filter(): jnp.einsum('aij,bjx->abix', band_matrix, cfield, preferred_element_type=j...  38.4 us
    dynamic_slice x64, local copies, waits for them, and re-layouts, local(): lax.scan(forward, jnp.zeros((row_count, col_count), jnp.float32), (row_ba...  38.3 us
    psum x1, waiting for transfers between devices, local(): summed_grad = lax.psum(gradient, 'corner')  37.5 us
  transfers between devices with their start and end apart: 6, of which 3 were waited for; matrix products, arithmetic and copies ran while one was open for 10% of the time, Pallas kernels for 0%

commit v1 on v0

--- a/solution.py
+++ b/solution.py
@@ -82,6 +82,11 @@
 
 
 def local(mask, target, pixel_weight, row_taps, col_taps, kernel_weights, corner_set, dose):
+
+    def use_stacks_all(frame_in):
+        mid_arr = lax.all_gather(frame_in, axis_name="corner").sum(axis=0)
+        return mid_arr
+
     row_count, col_count = mask.shape
     reach_rows = (row_taps.shape[-1] - 1) // 2
     set_count = row_taps.shape[0]
@@ -150,7 +155,7 @@
     first_row = lax.axis_index("corner") * share_rows
     own_mask = lax.dynamic_slice_in_dim(mask, first_row, share_rows, 0)
     pixel_count = row_count * lax.axis_size("tile") * col_count
-    summed_grad = lax.psum(gradient, "corner")
+    summed_grad = use_stacks_all(gradient)
     square = lax.psum(jnp.sum(summed_grad * summed_grad), "tile")
     own_rows = lax.dynamic_slice_in_dim(summed_grad, first_row, share_rows, 0)
     root_mean = jnp.sqrt(square / pixel_count + small_eps)

time: 598 us -> 580 us (0.970)
  waiting for transfers between devices: 71.6 us -> 33.6 us
  blocking collectives: 12.4 us -> 32.7 us
    psum x1 -> x0, waiting for transfers between devices: 37.5 us -> none  [local(): summed_grad = lax.psum(gradient, 'corner')]
    all_gather x0 -> x1, blocking collectives: none -> 17.9 us  [use_stacks_all(): mid_arr = lax.all_gather(frame_in, axis_name='corner').sum(axis=0)]
    unnamed x51 -> x53, local copies, waits for them, and re-layouts: 11.5 us -> 12.4 us
  transfers between devices with their start and end apart: 6 -> 5, of which waited for: 3 -> 2; matrix products, arithmetic and copies ran while one was open for 10% -> 10% of each run, Pallas kernels for 0% -> 0%
where the time goes in v1:
time: 580 us; the launch traced here: 575 us
  other arithmetic  205 us (35%)
  matrix products  152 us (26%)
  local copies, waits for them, and re-layouts  123 us (21%)
  waiting for transfers between devices  33.6 us (6%)
  blocking collectives  32.7 us (6%)
  between operations  17.7 us (3%)
  starting transfers between devices  6.88 us (1%)
    add x32, other arithmetic, forward(): running + kernel_weight * (field_real * field_real + field_imag * field_i...  48.1 us
    another operation x129, other arithmetic  47.1 us
    scatter-add x64, other arithmetic, column_adjoint(): summed.at[:, b * block_cols:b * block_cols + block_cols + 2 * reach_cols]  45.6 us
    dot_general x32, matrix products, row_adjoint(): jnp.einsum('aij,bix->abjx', band_matrix, cotangent, preferred_element_typ...  43.4 us
    dot_general x32, matrix products, column_filter(): jnp.einsum('bri,poi->prbo', windows, band_matrix, preferred_element_type=...  38.8 us
    dynamic_slice x64, local copies, waits for them, and re-layouts, local(): lax.scan(forward, jnp.zeros((row_count, col_count), jnp.float32), (row_ba...  38.4 us
    dot_general x32, matrix products, row_filter(): jnp.einsum('aij,bjx->abix', band_matrix, cfield, preferred_element_type=j...  38.4 us
    another operation x16, local copies, waits for them, and re-layouts, toeplitz(): repeated = jnp.tile(padded, (1,) * len(leading) + (row_count,))  32.5 us
  transfers between devices with their start and end apart: 5, of which 2 were waited for; matrix products, arithmetic and copies ran while one was open for 10% of the time, Pallas kernels for 0%

profile of v1, /device:TPU:0, one launch (start us, length us, event | category | flops | bytes accessed | tf_op | source)
XLA Modules:
  0.0 574.9 jit_solution(1574689321029557206)
XLA Ops:
  9.4 3.0 collective-permute-start
  27.0 3.1 tile.39
  32.8 3.1 tile.81
  38.5 3.1 tile.83
  44.1 3.1 tile.85
  50.8 3.1 tile.87
  56.5 3.1 tile.33
  62.1 3.1 tile.35
  68.8 49.1 %while.133 = (s32[]{:T(128)}, f32[128,384]{0,1:T(8,128)}, bf16[8,2,128,384]{2,3,0,1:T(8,128)(2,1)}, f32[8]{0:T(128)S(1)}, bf16[8,2,128,256]{3,2,1,0:T(8,128)(2,1...) while((s32[]{:T(128)}, f32[128,384]{0,1:T(8,128)}, ...), condition=%wide.region_9.10_spmd.clone, body=%wide.region_8.9_spmd.clone.sunk | while | flops 203685888 | bytes 5506679 | solution.py:113
  78.1 2.3 bitcast_add_fusion.9
  84.4 2.3 bitcast_add_fusion.9
  121.1 49.0 %while.134 = (s32[]{:T(128)}, f32[128,384]{0,1:T(8,128)}, bf16[8,2,128,384]{2,3,0,1:T(8,128)(2,1)}, f32[8]{0:T(128)S(1)}, bf16[8,2,128,256]{3,2,1,0:T(8,128)(2,1...) while((s32[]{:T(128)}, f32[128,384]{0,1:T(8,128)}, ...), condition=%wide.region_14.15_spmd.clone, body=%wide.region_13.14_spmd.clone.sunk | while | flops 203685888 | bytes 5506679 | solution.py:113
  173.4 38.2 %while.135 = (s32[]{:T(128)}, f32[128,384]{0,1:T(8,128)S(1)}, bf16[8,2,128,384]{2,3,0,1:T(8,128)(2,1)}, f32[8]{0:T(128)S(1)}, bf16[8,2,128,256]{3,2,1,0:T(8,128)...) while((s32[]{:T(128)}, f32[128,384]{0,1:T(8,128)S(1)}, ...), condition=%wide.region_19.20_spmd.clone, body=%wide.region_18.19_spmd.clone.sunk | while | flops 203685888 | bytes 5506679 | solution.py:113
  213.8 38.2 %while.132 = (s32[]{:T(128)}, f32[128,384]{0,1:T(8,128)S(1)}, bf16[8,2,128,384]{2,3,0,1:T(8,128)(2,1)}, f32[8]{0:T(128)S(1)}, bf16[8,2,128,256]{3,2,0,1:T(8,128)...) while((s32[]{:T(128)}, f32[128,384]{0,1:T(8,128)S(1)}, ...), condition=%wide.region_4.5_spmd.clone, body=%wide.region_3.4_spmd.clone.sunk | while | flops 203685888 | bytes 5506679 | solution.py:113
  252.1 4.8 add_convert_fusion
  264.7 30.7 %all-reduce.20.cloned.1.call-done = bf16[128,384]{1,0:T(8,128)(2,1)} async-done(((bf16[128,384]{1,0:T(8,128)(2,1)}), bf16[128,384]{1,0:T(8,128)(2,1)}) %all-reduce.20.cloned.1.call-update) | async-done | bytes 98320 | tf_op jit(solution)/shard_map/psum | solution.py:122
  295.4 4.9 fusion.160
  300.5 57.2 %while.136 = (s32[]{:T(128)}, f32[256,384]{0,1:T(8,128)S(1)}, bf16[8,2,128,256]{3,2,0,1:T(8,128)(2,1)}, f32[8]{0:T(128)S(1)}, f32[128,384]{0,1:T(8,128)S(1)}, /*...) while((s32[]{:T(128)}, f32[256,384]{0,1:T(8,128)S(1)}, ...), condition=%wide.region_25.26_spmd.clone, body=%wide.region_23.25_spmd.clone.sunk | while | flops 203374592 | bytes 10618519 | solution.py:143
  358.7 56.9 %while.129 = (s32[]{:T(128)}, f32[256,384]{0,1:T(8,128)S(1)}, bf16[8,2,128,256]{2,3,1,0:T(8,128)(2,1)}, f32[8]{0:T(128)S(1)}, f32[128,384]{0,1:T(8,128)S(1)}, /*...) while((s32[]{:T(128)}, f32[256,384]{0,1:T(8,128)S(1)}, ...), condition=%wide.region_28.29_spmd, body=%wide.region_26.28_spmd.sunk | while | flops 203276288 | bytes 10618501 | solution.py:143
  416.7 57.0 %while.130 = (s32[]{:T(128)}, f32[256,384]{0,1:T(8,128)S(1)}, bf16[8,2,128,256]{2,3,1,0:T(8,128)(2,1)}, f32[8]{0:T(128)S(1)}, f32[128,384]{0,1:T(8,128)S(1)}, /*...) while((s32[]{:T(128)}, f32[256,384]{0,1:T(8,128)S(1)}, ...), condition=%wide.region_31.32_spmd, body=%wide.region_29.31_spmd.sunk | while | flops 203276288 | bytes 10618501 | solution.py:143
  473.8 51.8 %while.131 = (s32[]{:T(128)}, f32[256,384]{0,1:T(8,128)S(1)}, bf16[8,2,128,256]{2,3,1,0:T(8,128)(2,1)S(1)}, f32[8]{0:T(128)S(1)}, f32[128,384]{0,1:T(8,128)S(1)}...) while((s32[]{:T(128)}, f32[256,384]{0,1:T(8,128)S(1)}, ...), condition=%wide.region_34.35_spmd, body=%wide.region_32.34_spmd.sunk | while | flops 203276288 | bytes 10617993 | solution.py:143
  529.2 2.9 collective-permute-done.3
  532.3 17.9 %all-gather = f32[512,384]{0,1:T(8,128)S(1)} all-gather(f32[128,384]{0,1:T(8,128)S(1)} %pad_add_fusion), channel_id=2, replica_groups=mesh['tile'=8,'corner'=4] {'corner'}, dimensions={0}, use_global_device_ids=true | all-gather | bytes 983040 | tf_op jit(solution)/shard_map/all_gather | solution.py:87
  551.7 14.8 %psum.15 = f32[]{:T(128)} all-reduce(f32[]{:T(128)} %multiply_reduce_fusion), channel_id=1, replica_groups=mesh['tile'=8,'corner'=4] {'tile'}, use_global_device_ids=true, to_apply=%region_37.38 | all-reduce | flops 1 | bytes 8 | tf_op jit(solution)/shard_map/psum | solution.py:159
  (760 shorter events, 448.6 us)
Async XLA Ops:
  7.2 288.2 %all-reduce.20.cloned.1.call-start = ((), (), s32[]{:S(2)}) async-start(), calls=%async_computation | async-start | bytes 196608 | tf_op jit(solution)/shard_map/psum | solution.py:122
  8.2 0.6 copy-start.7
  9.4 57.1 %collective-permute-start = (bf16[64,384]{1,0:T(8,128)(2,1)}, bf16[64,384]{1,0:T(8,128)(2,1)}, u32[]{:S(2)}, u32[]{:S(2)}) collective-permute-start(bf16[64,384]{1,0:T(8,128)(2,1)} %get-tuple-element.1632), channel_id=1, source_target_pairs={{0,4},{4,8},{8,12},{12,16},{16,20},{20,24},{24,28},{1,5},{5,9},{9,... | collective-permute-start | bytes 147464 | tf_op jit(solution)/shard_map/ppermute | solution.py:21
  12.4 54.1 %collective-permute-start.1 = (bf16[64,384]{1,0:T(8,128)(2,1)}, bf16[64,384]{1,0:T(8,128)(2,1)}, u32[]{:S(2)}, u32[]{:S(2)}) collective-permute-start(bf16[64,384]{1,0:T(8,128)(2,1)} %get-tuple-element.1633), channel_id=1, source_target_pairs={{4,0},{8,4},{12,8},{16,12},{20,16},{24,20},{28,24},{5,1},{9,5},{13... | collective-permute-start | bytes 147464 | tf_op jit(solution)/shard_map/ppermute | solution.py:22
  30.1 1.3 copy-start.13
  35.9 1.3 copy-start.12
  41.6 1.2 copy-start.11
  47.3 1.0 copy-start
  48.3 1.2 copy-start.10
  53.9 1.2 copy-start.9
  65.3 1.2 copy-start.8
  65.3 3.5 copy-start.15
  117.9 3.2 copy-start.14
  211.6 2.3 copy-start.16
  252.1 6.7 %copy-start.5 = (f32[128,384]{1,0:T(8,128)}, f32[128,384]{1,0:T(8,128)S(1)}, u32[]{:S(2)}) copy-start(f32[128,384]{1,0:T(8,128)S(1)} %copy.82) | copy-start | bytes 589828
  261.2 1.7 copy-start.1
  263.0 32.4 %copy-start.2 = (f32[128,384]{1,0:T(8,128)S(1)}, f32[128,384]{1,0:T(8,128)}, u32[]{:S(2)}) copy-start(f32[128,384]{1,0:T(8,128)} %copy.87) | copy-start | bytes 589828
  263.0 32.4 %copy-start.3 = (f32[128,384]{1,0:T(8,128)S(1)}, f32[128,384]{1,0:T(8,128)}, u32[]{:S(2)}) copy-start(f32[128,384]{1,0:T(8,128)} %copy.92) | copy-start | bytes 589828
  263.0 32.4 %copy-start.4 = (f32[128,384]{1,0:T(8,128)S(1)}, f32[128,384]{1,0:T(8,128)}, u32[]{:S(2)}) copy-start(f32[128,384]{1,0:T(8,128)} %copy.97) | copy-start | bytes 589828
  263.0 32.4 %copy-start.6 = (f32[128,384]{1,0:T(8,128)S(1)}, f32[128,384]{1,0:T(8,128)}, u32[]{:S(2)}) copy-start(f32[128,384]{1,0:T(8,128)} %copy-done.5) | copy-start | bytes 589828
  525.8 3.4 collective-permute-start.2
  527.1 5.0 collective-permute-start.3
Sparse Core Ops, SparseCore 0:
  257.1 38.3 all-reduce.19
